TPU v7x, 32 devices: a whole 2x2x4 slice. The times are simulated.
32 devices in a mesh: section: 2 (over core), dp: 16 (over z, y, x).
Axes of the slice: x: 2, y: 2, z: 4, core: 2. Of those that a mesh axis runs over, the one named last changes fastest.
Arguments:
- hidden: bfloat16 [16384, 768], P('dp'), may hold values from -6 to 6
- segment_ids: int32 [32, 512], P('dp'), may hold values from 0 to 3, never falling along the last dimension, each value on 1 to 256 neighbouring positions
- cotangent: bfloat16 [2, 16384, 768], P('section', 'dp'), may hold values from -6 to 6
- w_qkv: bfloat16 [2, 768, 2304], P('section'), may hold values from -0.21875 to 0.21875
- w_out: bfloat16 [2, 768, 768], P('section'), may hold values from -2.5 to 2.5
- w_up: bfloat16 [2, 768, 3072], P('section'), may hold values from -0.21875 to 0.21875
- w_down: bfloat16 [2, 3072, 768], P('section'), may hold values from -0.109375 to 0.109375
- biases: float32 [2, 6, 768], P('section'), may hold values from -3 to 3
- gains: float32 [2, 2, 768], P('section'), may hold values from 0.25 to 1.75
- up_bias: float32 [2, 3072], P('section'), may hold values from -3 to 3
Outputs:
- states: bfloat16 [2, 16384, 768], P('section', 'dp')
- grad_input: float32 [16384, 768], P('dp')
- grad_w_qkv: float32 [2, 768, 2304], P('section', 'dp')
- grad_w_out: float32 [2, 768, 768], P('section', 'dp')
- grad_w_up: float32 [2, 768, 3072], P('section', 'dp')
- grad_w_down: float32 [2, 3072, 768], P('section', 'dp')
- grad_biases: float32 [2, 6, 768], P('section', None, 'dp')
- grad_gains: float32 [2, 2, 768], P('section', None, 'dp')
- grad_up_bias: float32 [2, 3072], P('section', 'dp')
Inputs may be any that keep to these rules, and one draw needn't show every extreme that they name: `segment_ids`: in every sequence the ids run through 0 to 3 without falling, each document 1 to 256 tokens, one exactly 256.
All inputs are finite; a program needn't handle non-finite values.
Results may differ from a plain program's by a relative error of at most 0.015.
Values may be sent and summed in bfloat16 or wider, within the bound.
A program may use at most 256 MiB of HBM per device.

v0:
```python
import functools

import jax
import jax.numpy as jnp
from jax import lax
from jax.experimental import pallas as pl
from jax.experimental.pallas import tpu as pltpu
from jax.sharding import PartitionSpec as P

HEADS = 12
HEAD = 64
NORM_EPS = 1e-12
MASKED = -1e30
INV_ROOT_TWO = 0.7071067811865476
INV_ROOT_TAU = 0.3989422804014327
MESH = pl.DeviceIdType.MESH
BF = jnp.bfloat16
F32 = jnp.float32
TILE = 256
ROWS = 128
VMEM_BYTES = 60 * 1024 * 1024


def dot_nn(a, b):
    return lax.dot_general(a, b, (((1,), (0,)), ((), ())), preferred_element_type=F32)


def dot_nt(a, b):
    return lax.dot_general(a, b, (((1,), (1,)), ((), ())), preferred_element_type=F32)


def dot_tn(a, b):
    return lax.dot_general(a, b, (((0,), (0,)), ((), ())), preferred_element_type=F32)


def loop(count, body, unroll=1):
    def step(i, carry):
        body(i)
        return carry

    lax.fori_loop(0, count, step, 0, unroll=unroll)


def tile_of(i, size=TILE):
    return pl.ds(pl.multiple_of(i * size, size), size)


class Weights:
    def __init__(self, block, pairs, targets, sems):
        self.waits = []
        own = lax.axis_index("section") == block
        for n, ((mine, theirs), target) in enumerate(zip(pairs, targets)):
            sem = sems.at[n]

            @pl.when(own)
            def _():
                pltpu.make_async_copy(mine, target, sem).start()

            @pl.when(jnp.logical_not(own))
            def _():
                pltpu.make_async_copy(theirs, target, sem).start()

            self.waits.append(pltpu.make_async_copy(mine, target, sem))

    def wait(self, n):
        self.waits[n].wait()


def normed_rows(residue):
    centered = residue - jnp.mean(residue, axis=-1, keepdims=True)
    inv = lax.rsqrt(jnp.mean(centered * centered, axis=-1, keepdims=True) + NORM_EPS)
    return centered * inv, inv


def lane_masks(shape):
    lane = lax.broadcasted_iota(jnp.int32, shape, 1)
    return (lane < HEAD, lane >= HEAD)


def spread_marks(seg_ref, sec, mask_ref, first_ref):
    rows = mask_ref.shape[0]
    line = jnp.where(sec == 0, seg_ref[0:1, :], seg_ref[1:2, :]).astype(F32)
    column = jnp.broadcast_to(line, (128, rows)).T
    mask_ref[...] = jnp.where(column[:, 0:1] == line, 0.0, MASKED)
    lines = jnp.broadcast_to(line, (8, rows))
    before = pltpu.roll(lines, 1, 1)
    lane = lax.broadcasted_iota(jnp.int32, (8, rows), 1)
    marks = jnp.where((lines != before) | (lane == 0), 1.0, 0.0)
    first_ref[...] = jnp.broadcast_to(marks[0:1, :], (128, rows)).T


def weight_piece(refs, n, width):
    wqkv, wout, wup, wdown = refs
    if n < 3:
        return wqkv.at[0, :, pl.ds(n * width, width)]
    if n < 4:
        return wout.at[0]
    count = wdown.shape[1] // width
    if n < 4 + count:
        return wup.at[0, :, pl.ds((n - 4) * width, width)]
    return wdown.at[0, pl.ds((n - 4 - count) * width, width), :]


def forward_kernel(*refs):
    hidden, seg_ref, cotangent = refs[0:3]
    own_weights = refs[3:7]
    biases_ref, gains_ref, upb_ref = refs[7:10]
    (qkv_out, o_out, lse_out, n1_out, inv1_out, hlow_out, g_out, slope_out, n2_out, inv2_out,
     x1_out, states_out, theirs_out, cot_out, smalls) = refs[10:25]
    (wbuf, x_buf, qkv_buf, o_buf, lse_buf, n1_buf, inv1_buf, hlow_buf, g_buf, slope_buf, n2_buf, inv2_buf, y_buf,
     res, h_buf, mask_ref, first_ref,
     own_sem, piece_send, piece_recv, keep_sem, out_sem, x_sem, misc_send, misc_recv) = refs[25:]
    rows, width = x_buf.shape
    pieces = wbuf.shape[1]
    count = (pieces - 4) // 2
    sec = lax.axis_index("section")
    mine = pl.ds(pl.multiple_of(sec * rows, rows), rows)
    others = pl.ds(pl.multiple_of((1 - sec) * rows, rows), rows)
    partner = {"section": 1 - sec}

    def own_piece(n):
        return pltpu.make_async_copy(weight_piece(own_weights, n, width), wbuf.at[sec, n], own_sem.at[n])

    def sent_piece(n, block):
        return pltpu.make_async_remote_copy(
            src_ref=weight_piece(own_weights, n, width), dst_ref=wbuf.at[block, n],
            send_sem=piece_send.at[n], recv_sem=piece_recv.at[n], device_id=partner, device_id_type=MESH,
        )

    def kept_piece(n):
        return pltpu.make_async_copy(wbuf.at[1 - sec, n], theirs_out.at[n], keep_sem.at[n])

    def sent_small():
        return pltpu.make_async_remote_copy(
            src_ref=smalls.at[sec], dst_ref=smalls.at[sec],
            send_sem=misc_send.at[0], recv_sem=misc_recv.at[0], device_id=partner, device_id_type=MESH,
        )

    def sent_cot():
        return pltpu.make_async_remote_copy(
            src_ref=cotangent.at[0, others], dst_ref=cot_out,
            send_sem=misc_send.at[1], recv_sem=misc_recv.at[1], device_id=partner, device_id_type=MESH,
        )

    def sent_state(b):
        return pltpu.make_async_remote_copy(
            src_ref=y_buf.at[b], dst_ref=states_out.at[mine],
            send_sem=misc_send.at[2], recv_sem=misc_recv.at[2], device_id=partner, device_id_type=MESH,
        )

    def own_state(b):
        return pltpu.make_async_copy(y_buf.at[b], states_out.at[mine], x_sem.at[1])

    def piece(b, n):
        @pl.when(sec == b)
        def _():
            own_piece(n).wait()

        @pl.when(sec != b)
        def _():
            sent_piece(n, b).wait_recv()
            kept_piece(n).start()

        return wbuf.at[b, n]

    barrier = pltpu.get_barrier_semaphore()
    pl.semaphore_signal(barrier, inc=1, device_id=partner, device_id_type=MESH)
    load_x = pltpu.make_async_copy(hidden.at[mine], x_buf, x_sem.at[0])
    load_x.start()
    for n in range(pieces):
        own_piece(n).start()
    smalls[sec, 0:6, :] = biases_ref[0]
    smalls[sec, 6:8, :] = gains_ref[0]
    for j in range(count):
        smalls[sec, 8 + j : 9 + j, :] = upb_ref[:, j * width : (j + 1) * width]
    smalls[sec, 8 + count :, :] = jnp.zeros((smalls.shape[1] - 8 - count, width), F32)
    pl.semaphore_wait(barrier, 1)
    sent_small().start()
    for n in range(pieces):
        sent_piece(n, sec).start()
    sent_cot().start()
    spread_marks(seg_ref, sec, mask_ref, first_ref)
    load_x.wait()
    sent_small().wait()

    buffers = (
        (qkv_buf, qkv_out), (o_buf, o_out), (lse_buf, lse_out), (n1_buf, n1_out), (inv1_buf, inv1_out),
        (hlow_buf, hlow_out), (g_buf, g_out), (slope_buf, slope_out), (n2_buf, n2_out), (inv2_buf, inv2_out),
    )
    QKV, O, LSE, N1, INV1, HLOW, G, SLOPE, N2, INV2 = range(10)

    def stored(b, which):
        return pltpu.make_async_copy(buffers[which][0], buffers[which][1].at[b], out_sem.at[which])

    def store(b, *names):
        for which in names:
            stored(b, which).start()

    def free(b, *names):
        if b == 1:
            for which in names:
                stored(0, which).wait()

    for b in range(2):
        small = smalls.at[b]
        free(b, QKV)
        for n in range(3):
            block = piece(b, n)

            def project(t):
                cols = tile_of(t)
                there = pl.ds(pl.multiple_of(n * width + t * TILE, TILE), TILE)
                value = dot_nn(x_buf[...], block[:, cols])
                if n == 0:
                    value = (value + small[0:1, cols]) * (HEAD ** -0.5)
                elif n == 2:
                    value = value + small[1:2, cols]
                qkv_buf[:, there] = value.astype(BF)

            loop(width // TILE, project, 3)
        store(b, QKV)
        free(b, O, LSE)

        def attend(pair):
            queries = qkv_buf[:, tile_of(pair, 128)]
            keys = qkv_buf[:, pl.ds(pl.multiple_of(width + pair * 128, 128), 128)]
            values = qkv_buf[:, pl.ds(pl.multiple_of(2 * width + pair * 128, 128), 128)]
            masks = lane_masks((rows, 128))
            parts = []
            for h in range(2):
                scores = dot_nt(keys, jnp.where(masks[h], queries, jnp.zeros_like(queries))) + mask_ref[...]
                top = jnp.max(scores, axis=0, keepdims=True)
                weight = jnp.exp(scores - top)
                total = jnp.sum(weight, axis=0, keepdims=True)
                lse_buf[pair, pl.ds(h, 1), :] = top + jnp.log(total)
                result = dot_tn(values, weight.astype(BF))
                parts.append(result[h * HEAD : (h + 1) * HEAD] * (1.0 / total))
            o_buf[:, tile_of(pair, 128)] = jnp.concatenate(parts, axis=0).T.astype(BF)

        loop(HEADS // 2, attend, 2)
        store(b, O, LSE)
        mixer = piece(b, 3)

        def mix(t):
            cols = tile_of(t)
            res[:, cols] = x_buf[:, cols].astype(F32) + (dot_nn(o_buf[...], mixer[:, cols]) + small[2:3, cols])

        loop(width // TILE, mix, 3)
        free(b, N1, INV1, HLOW)

        def norm_one(i):
            r = tile_of(i, ROWS)
            normed, inv = normed_rows(res[r, :])
            n1_buf[r, :] = normed
            inv1_buf[r, :] = jnp.broadcast_to(inv, (ROWS, 128))
            h = normed * small[6:7, :] + small[3:4, :]
            h_buf[r, :] = h + small[4:5, :]
            hlow_buf[r, :] = h.astype(BF)

        loop(rows // ROWS, norm_one, 2)
        store(b, N1, INV1, HLOW)
        free(b, G, SLOPE)
        for j in range(count):
            up = piece(b, 4 + j)

            def widen(t):
                cols = tile_of(t)
                there = pl.ds(pl.multiple_of(j * width + t * TILE, TILE), TILE)
                z = dot_nn(hlow_buf[...], up[:, cols]) + small[8 + j : 9 + j, cols]
                half = 0.5 * (1.0 + lax.erf(z * INV_ROOT_TWO))
                g_buf[:, there] = (z * half).astype(BF)
                slope_buf[:, there] = (half + z * jnp.exp(-0.5 * z * z) * INV_ROOT_TAU).astype(BF)

            loop(width // TILE, widen, 3)
        store(b, G, SLOPE)
        for j in range(count):
            down = piece(b, 4 + count + j)

            def narrow(t):
                cols = tile_of(t)
                h_buf[:, cols] += dot_nn(g_buf[:, j * width : (j + 1) * width], down[:, cols])

            loop(width // TILE, narrow, 3)
        free(b, N2, INV2)

        def norm_two(i):
            r = tile_of(i, ROWS)
            normed, inv = normed_rows(h_buf[r, :])
            n2_buf[r, :] = normed
            inv2_buf[r, :] = jnp.broadcast_to(inv, (ROWS, 128))
            y = (normed * small[7:8, :] + small[5:6, :]).astype(BF)
            y_buf[b, r, :] = y
            if b == 0:
                x = x_buf[r, :].astype(F32)
                x_buf[r, :] = jnp.where(first_ref[r, 0:1] > 0.5, y.astype(F32), x).astype(BF)

        loop(rows // ROWS, norm_two, 2)
        store(b, N2, INV2)
        if b == 0:
            pltpu.make_async_copy(x_buf, x1_out, x_sem.at[0]).start()

        @pl.when(sec == b)
        def _():
            own_state(b).start()

        @pl.when(sec != b)
        def _():
            sent_state(b).start()

    for which in range(10):
        stored(1, which).wait()
    pltpu.make_async_copy(x_buf, x1_out, x_sem.at[0]).wait()
    own_state(0).wait()
    sent_state(0).wait()
    sent_cot().wait()
    for n in range(pieces):
        sent_piece(n, sec).wait_send()
        kept_piece(n).wait()


def norm_back(gradient, normed, inv):
    return inv * (
        gradient
        - jnp.mean(gradient, axis=-1, keepdims=True)
        - normed * jnp.mean(gradient * normed, axis=-1, keepdims=True)
    )


def column_sum(v):
    return jnp.sum(v, axis=0, keepdims=True)


def backward_kernel(
    block,
    cot_ref, dnext_ref, segr_ref, segc_ref, first_ref, small_ref,
    qkv_ref, o_ref, lse_ref, n1_ref, inv1_ref, slope_ref, n2_ref, inv2_ref,
    wqkv_m, wqkv_t, wout_m, wout_t, wup_m, wup_t, wdown_m, wdown_t,
    dx_ref, dproj_ref, da_ref, dz_ref, df_ref, dsmall_ref, dup_ref,
    wqkv, wout, wup, wdown, mask_ref, dr_ref, dh_ref, do_ref, sems,
):
    rows, width = cot_ref.shape
    hidden_width = wup.shape[1]
    weights = Weights(
        block,
        ((wdown_m, wdown_t), (wup_m, wup_t), (wout_m, wout_t), (wqkv_m, wqkv_t)),
        (wdown, wup, wout, wqkv),
        sems,
    )
    mask_ref[...] = jnp.where(segc_ref[...] == segr_ref[...], 0.0, MASKED)
    dsmall_ref[...] = jnp.zeros_like(dsmall_ref)

    def norm_two(i):
        r = tile_of(i, ROWS)
        gradient = cot_ref[r, :].astype(F32)
        if block == 0:
            back = dnext_ref[r, :].astype(BF).astype(F32)
            gradient = gradient + jnp.where(first_ref[r, :] > 0.5, back, 0.0)
        normed = n2_ref[r, :]
        dr = norm_back(gradient * small_ref[7:8, :], normed, inv2_ref[r, 0:1])
        dr_ref[r, :] = dr
        df_ref[r, :] = dr.astype(BF)
        dsmall_ref[7:8, :] += column_sum(gradient * normed)
        dsmall_ref[5:6, :] += column_sum(gradient)
        dsmall_ref[4:5, :] += column_sum(dr)

    loop(rows // ROWS, norm_two, 2)
    weights.wait(0)

    def narrow(j):
        cols = tile_of(j)
        dz = dot_nt(df_ref[...], wdown[cols, :]) * slope_ref[:, cols].astype(F32)
        dup_ref[:, cols] = column_sum(dz)
        dz_ref[:, cols] = dz.astype(BF)

    loop(hidden_width // TILE, narrow)
    weights.wait(1)

    def widen(j):
        cols = tile_of(j)
        dh_ref[:, cols] = dr_ref[:, cols] + dot_nt(dz_ref[...], wup[cols, :])

    loop(width // TILE, widen, 3)

    def norm_one(i):
        r = tile_of(i, ROWS)
        gradient = dh_ref[r, :]
        normed = n1_ref[r, :]
        dr = norm_back(gradient * small_ref[6:7, :], normed, inv1_ref[r, 0:1])
        dr_ref[r, :] = dr
        da_ref[r, :] = dr.astype(BF)
        dsmall_ref[6:7, :] += column_sum(gradient * normed)
        dsmall_ref[3:4, :] += column_sum(gradient)
        dsmall_ref[2:3, :] += column_sum(dr)

    loop(rows // ROWS, norm_one, 2)
    weights.wait(2)

    def mix(j):
        cols = tile_of(j)
        do_ref[:, cols] = dot_nt(da_ref[...], wout[cols, :]).astype(BF)

    loop(width // TILE, mix, 3)

    def attend(pair):
        here = tile_of(pair, 128)
        key_cols = pl.ds(pl.multiple_of(width + pair * 128, 128), 128)
        value_cols = pl.ds(pl.multiple_of(2 * width + pair * 128, 128), 128)
        queries, keys, values = qkv_ref[:, here], qkv_ref[:, key_cols], qkv_ref[:, value_cols]
        grad = do_ref[:, here]
        masks = lane_masks((rows, 128))
        dq, dk, dv = [], 0.0, 0.0
        for h in range(2):
            head_queries = jnp.where(masks[h], queries, jnp.zeros_like(queries))
            head_grad = jnp.where(masks[h], grad, jnp.zeros_like(grad))
            scores = dot_nt(keys, head_queries) + mask_ref[...]
            weight = jnp.exp(scores - lse_ref[pair, pl.ds(h, 1), :])
            dweight = dot_nt(values, head_grad)
            delta = jnp.sum(weight * dweight, axis=0, keepdims=True)
            dscore = (weight * (dweight - delta)).astype(BF)
            dq.append(dot_tn(keys, dscore)[h * HEAD : (h + 1) * HEAD])
            dk = dk + dot_nn(dscore, head_queries)
            dv = dv + dot_nn(weight.astype(BF), head_grad)
        dq = jnp.concatenate(dq, axis=0).T * (HEAD ** -0.5)
        dsmall_ref[0:1, here] = column_sum(dq)
        dsmall_ref[1:2, here] = column_sum(dv)
        dproj_ref[:, here] = dq.astype(BF)
        dproj_ref[:, key_cols] = dk.astype(BF)
        dproj_ref[:, value_cols] = dv.astype(BF)

    loop(HEADS // 2, attend)
    weights.wait(3)

    def project(j):
        cols = tile_of(j)
        dx = dr_ref[:, cols] + dot_nt(dproj_ref[...], wqkv[cols, :])
        if block == 0:
            dx = dx + jnp.where(first_ref[...] > 0.5, 0.0, dnext_ref[:, cols])
        dx_ref[:, cols] = dx

    loop(width // TILE, project, 3)


def in_vmem(count):
    return [pl.BlockSpec(memory_space=pltpu.VMEM)] * count


def in_hbm(count):
    return [pl.BlockSpec(memory_space=pl.ANY)] * count


def shaped(shape, dtype=F32):
    return jax.ShapeDtypeStruct(shape, dtype)


def both_forward(hidden, seg, cotangent, weights, biases, gains, up_bias):
    rows, width = hidden.shape[0] // 2, hidden.shape[1]
    hidden_width = up_bias.shape[1]
    pieces = 2 * hidden_width // width + 4
    kept = (
        ((rows, 3 * width), BF), ((rows, width), BF), ((HEADS // 2, 2, rows), F32), ((rows, width), F32),
        ((rows, 128), F32), ((rows, width), BF), ((rows, hidden_width), BF), ((rows, hidden_width), BF),
        ((rows, width), F32), ((rows, 128), F32),
    )
    return pl.pallas_call(
        forward_kernel,
        out_shape=tuple(shaped((2,) + shape, dtype) for shape, dtype in kept) + (
            shaped((rows, width), BF), shaped((2 * rows, width), BF), shaped((pieces, width, width), BF),
            shaped((rows, width), BF), shaped((2, 16, width)),
        ),
        in_specs=in_hbm(1) + in_vmem(1) + in_hbm(1) + in_hbm(4) + in_vmem(3),
        out_specs=tuple(in_hbm(14) + in_vmem(1)),
        scratch_shapes=[
            pltpu.VMEM((2, pieces, width, width), BF),
            pltpu.VMEM((rows, width), BF),
        ] + [pltpu.VMEM(shape, dtype) for shape, dtype in kept] + [
            pltpu.VMEM((2, rows, width), BF),
            pltpu.VMEM((rows, width), F32),
            pltpu.VMEM((rows, width), F32),
            pltpu.VMEM((rows, rows), F32),
            pltpu.VMEM((rows, 128), F32),
            pltpu.SemaphoreType.DMA((pieces,)),
            pltpu.SemaphoreType.DMA((pieces,)),
            pltpu.SemaphoreType.DMA((pieces,)),
            pltpu.SemaphoreType.DMA((pieces,)),
            pltpu.SemaphoreType.DMA((10,)),
            pltpu.SemaphoreType.DMA((2,)),
            pltpu.SemaphoreType.DMA((3,)),
            pltpu.SemaphoreType.DMA((3,)),
        ],
        compiler_params=pltpu.CompilerParams(
            collective_id=1, has_side_effects=True, vmem_limit_bytes=VMEM_BYTES
        ),
        name="forward",
    )(hidden, seg, cotangent, *weights, biases, gains, up_bias)


def block_backward(block, cot, dnext, segr, segc, first, small, kept, weights):
    rows, width = cot.shape
    hidden_width = weights[4].shape[1]
    scratch = [pltpu.VMEM(w.shape, BF) for w in weights[::2]]
    return pl.pallas_call(
        functools.partial(backward_kernel, block),
        out_shape=(
            shaped((rows, width)), shaped((rows, 3 * width), BF), shaped((rows, width), BF),
            shaped((rows, hidden_width), BF), shaped((rows, width), BF), shaped((16, width)), shaped((1, hidden_width)),
        ),
        in_specs=in_vmem(14) + in_hbm(8),
        out_specs=tuple(in_vmem(7)),
        scratch_shapes=scratch + [
            pltpu.VMEM((rows, rows), F32), pltpu.VMEM((rows, width), F32), pltpu.VMEM((rows, width), F32),
            pltpu.VMEM((rows, width), BF), pltpu.SemaphoreType.DMA((4,)),
        ],
        compiler_params=pltpu.CompilerParams(vmem_limit_bytes=VMEM_BYTES),
        name="backward" + str(block),
    )(cot, dnext, segr, segc, first, small, *kept, *weights)


ORDERS = {
    "A": (0, 1, 2, 3), "B": (1, 0, 2, 3), "C": (2, 3, 0, 1), "D": (2, 3, 1, 0), "E": (0, 2, 3, 1), "F": (1, 2, 3, 0),
}
BITS = 4
PARTS = 1 << BITS
SLOTS = 4
SEQUENCE = (8, 9, 10, 11, 4, 5, 6, 7, 3, 0, 1, 2)
KINDS = ("AFEBABABEFAB", "EFAFEFEFEFAF")
SCHEDULE = (
    1428, 1424, 1892, 1888, 2005, 2001, 2108, 2104, 2081, 2184, 2181, 2194, 2572, 2582, 2681, 2775,
    2771, 2844, 2850, 2973, 3046, 3043, 3145, 3312, 3450, 3431, 3533, 3700, 3838, 3896, 4093, 4160,
    4181, 4202, 4302, 4319, 4315, 4548, 4566, 4574, 4587, 4657, 4720, 4840, 4857, 4833, 4916, 4913,
    4946, 4975, 4951, 5016, 5029, 5050, 5026, 5420, 5417, 5589, 5586, 5606, 5699, 5802, 5785, 5779,
    5772, 5803, 5786, 5819, 5811, 5787, 5773, 5764, 5774, 5765, 5775, 5766, 5767, 5823, 5805, 5782,
    5788, 5799, 5783, 5760, 5806, 5789, 5768, 5761, 5807, 5790, 5769, 5762, 5791, 5763, 5770, 5771,
)


def owner(b, chunk):
    return (b + SEQUENCE.index(chunk)) % 2


def backward_sum_kernel(*refs):
    kept = refs[0:10]
    hidden, x1, cotangent, cot_theirs = refs[10:14]
    own_weights, theirs = refs[14:18], refs[18]
    seg_ref, smalls = refs[19:21]
    out_qkv, out_out, out_up, out_down, out_biases, out_gains, out_upb, grad_input = refs[21:29]
    (total, slots, stage, r1, r2, r3, r4, wring, gring, sring, lhs, turned, norm_buf, inv_buf, cot_buf, qkv_buf, lse_buf,
     low_buf, dz_buf, acc, dx_ref, mask_ref, first_ref, dsmall, small_sum, small_in,
     cross_send, cross_recv, done_send, done_recv, send, recv, small_send, small_recv, wsem, gsem, ssem, asem,
     grad_sem) = refs[29:]
    received = (r1, r2, r3, r4)
    rows, width = acc.shape
    share = total.shape[-2]
    wide = gring.shape[0]
    count = out_up.shape[1] // width
    sec, me = lax.axis_index("section"), lax.axis_index("dp")
    bits = [(me >> k) & 1 for k in range(BITS)]
    mine = pl.ds(pl.multiple_of(sec * rows, rows), rows)

    barrier = pltpu.get_barrier_semaphore()
    for k in range(BITS):
        pl.semaphore_signal(barrier, inc=1, device_id={"dp": me ^ (1 << k)}, device_id_type=MESH)
    pl.semaphore_signal(barrier, inc=1, device_id={"section": 1 - sec}, device_id_type=MESH)

    weight_list = []
    for b in (1, 0):
        for j in range(count):
            weight_list += [(b, 4 + count + j), (b, 4 + j)]
        weight_list += [(b, 3), (b, 0), (b, 1), (b, 2)]

    def weight_copy(n, own):
        which = weight_list[n][1]
        source = weight_piece(own_weights, which, width) if own else theirs.at[which]
        return pltpu.make_async_copy(source, wring.at[n % wring.shape[0]], wsem.at[n % wring.shape[0]])

    def weight_start(n):
        if n < len(weight_list):
            own = sec == weight_list[n][0]

            @pl.when(own)
            def _():
                weight_copy(n, True).start()

            @pl.when(jnp.logical_not(own))
            def _():
                weight_copy(n, False).start()

    taken = [0]

    def weight_next():
        n = taken[0]
        taken[0] += 1
        weight_copy(n, False).wait()
        return wring.at[n % wring.shape[0]]

    def weight_done():
        weight_start(taken[0] - 1 + wring.shape[0])

    QKV, O, LSE, N1, INV1, HLOW, G, SLOPE, N2, INV2, COT, X = range(12)
    targets = {
        COT: (cot_buf, 0), QKV: (qkv_buf, 1), O: (lhs, 2), LSE: (lse_buf, 3), N1: (norm_buf, 4), INV1: (inv_buf, 5),
        HLOW: (lhs, 2), N2: (norm_buf, 4), INV2: (inv_buf, 5), X: (lhs, 2),
    }

    def act(b, which, own=False):
        target, sem = targets[which]
        if which == COT:
            source = cotangent.at[0, mine] if own else cot_theirs
        elif which == X:
            source = x1 if b == 1 else hidden.at[mine]
        else:
            source = kept[which].at[b]
        return pltpu.make_async_copy(source, target, asem.at[sem])

    def ring(b, which, j):
        buf, sem = (gring, gsem) if which == G else (sring, ssem)
        source = kept[which].at[b, :, pl.ds(j * width, width)]
        return pltpu.make_async_copy(source, buf.at[j % wide], sem.at[j % wide])

    def place(part):
        return tuple((part >> (BITS - 1 - k)) & 1 for k in range(BITS))

    def across(chunk, slot):
        return pltpu.make_async_remote_copy(
            src_ref=slots.at[slot], dst_ref=total.at[chunk],
            send_sem=cross_send.at[chunk], recv_sem=cross_recv.at[chunk],
            device_id={"section": 1 - sec}, device_id_type=MESH,
        )

    def hand_over(b, chunk, slot):
        @pl.when(sec != owner(b, chunk))
        def _():
            across(chunk, slot).start()

    def exchange(b, chunk, phase):
        order = ORDERS[KINDS[b][SEQUENCE.index(chunk)]]
        at = [slice(None)] * BITS
        for done in range(phase):
            at[BITS - 1 - order[done]] = bits[order[done]]
        at[BITS - 1 - order[phase]] = 1 - bits[order[phase]]
        return pltpu.make_async_remote_copy(
            src_ref=total.at[(chunk,) + tuple(at)], dst_ref=received[phase].at[chunk],
            send_sem=send.at[chunk, phase], recv_sem=recv.at[chunk, phase],
            device_id={"dp": me ^ (1 << order[phase])}, device_id_type=MESH,
        )

    def finish(b, chunk, slot):
        @pl.when(sec == owner(b, chunk))
        def _():
            across(chunk, slot).wait_recv()

            def one(i):
                at = (i // 8, (i // 4) % 2, (i // 2) % 2, i % 2)
                total[(chunk,) + at] = total[(chunk,) + at] + slots[(slot,) + at]

            loop(PARTS, one, 4)
            exchange(b, chunk, 0).start()

        @pl.when(sec != owner(b, chunk))
        def _():
            across(chunk, slot).wait_send()

    def result_of(chunk):
        if chunk < 3:
            return out_qkv.at[:, pl.ds(chunk * width, width)]
        if chunk < 4:
            return out_out
        if chunk < 8:
            return out_up.at[:, pl.ds((chunk - 4) * width, width)]
        return out_down.at[pl.ds((chunk - 8) * share, share), :]

    def bring(chunk):
        return pltpu.make_async_remote_copy(
            src_ref=stage.at[SEQUENCE.index(chunk) // 2], dst_ref=result_of(chunk),
            send_sem=done_send.at[chunk], recv_sem=done_recv.at[chunk],
            device_id={"section": 1 - sec}, device_id_type=MESH,
        )

    def take(b, chunk, phase):
        order = ORDERS[KINDS[b][SEQUENCE.index(chunk)]]
        exchange(b, chunk, phase).wait()

        def one(i):
            at, inner, left = [None] * BITS, [], i
            for done in range(phase + 1):
                at[BITS - 1 - order[done]] = bits[order[done]]
            for d in reversed([d for d in range(BITS) if at[d] is None]):
                at[d] = left % 2
                inner.insert(0, at[d])
                left = left // 2
            at = (chunk,) + tuple(at)
            total[at] = total[at] + received[phase][(chunk,) + tuple(inner)]

        if phase < BITS - 1:
            loop(PARTS >> (phase + 1), one, min(4, PARTS >> (phase + 1)))
            exchange(b, chunk, phase + 1).start()
        else:
            value = total[(chunk,) + tuple(bits[BITS - 1 - d] for d in range(BITS))].astype(F32)
            value = value + received[phase][chunk].astype(F32)
            if owner(b, chunk) == b:
                result_of(chunk)[...] = value
            else:
                stage[SEQUENCE.index(chunk) // 2] = value
                bring(chunk).start()

    steps = [(n // 96, (n // 48) % 2, (n // 4) % 12, n % 4) for n in SCHEDULE]
    points = [0]

    def run_steps(chosen):
        for core in range(2):
            mine = [step for step in chosen if owner(step[1], step[2]) == core]
            if mine:

                @pl.when(sec == core)
                def _():
                    for _, b, chunk, phase in mine:
                        take(b, chunk, phase)

    def point():
        run_steps([step for step in steps if step[0] == points[0]])
        points[0] += 1

    def product(right, right_col, put):
        def one(n):
            cols = tile_of(n)
            rhs_cols = pl.ds(pl.multiple_of(right_col + n * TILE, TILE), TILE)
            result = dot_nn(turned[...], right[:, rhs_cols]).astype(BF)
            for piece in range(PARTS):
                slot, part = put(piece)
                slots[(slot,) + place(part) + (slice(None), cols)] = result[piece * share : (piece + 1) * share]

        loop(width // TILE, one, 3)

    def first_loads(b):
        @pl.when(sec == b)
        def _():
            act(b, COT, True).start()

        @pl.when(sec != b)
        def _():
            act(b, COT).start()

        act(b, N2).start()
        act(b, INV2).start()
        for j in range(wide):
            ring(b, G, j).start()
            ring(b, SLOPE, j).start()

    first_loads(1)
    act(1, HLOW).start()
    for n in range(wring.shape[0]):
        weight_start(n)
    spread_marks(seg_ref, sec, mask_ref, first_ref)
    dsmall[...] = jnp.zeros_like(dsmall)

    for b in (1, 0):
        small = smalls.at[b]
        act(b, QKV).start()
        act(b, LSE).start()
        act(b, COT).wait()
        act(b, N2).wait()
        act(b, INV2).wait()

        def norm_two(i):
            r = tile_of(i, ROWS)
            gradient = cot_buf[r, :].astype(F32)
            if b == 0:
                back = dx_ref[r, :].astype(BF).astype(F32)
                gradient = gradient + jnp.where(first_ref[r, 0:1] > 0.5, back, 0.0)
            normed = norm_buf[r, :]
            dr = norm_back(gradient * small[7:8, :], normed, inv_buf[r, 0:1])
            acc[r, :] = dr
            low_buf[r, :] = dr.astype(BF)
            dsmall[b, 7:8, :] += column_sum(gradient * normed)
            dsmall[b, 5:6, :] += column_sum(gradient)
            dsmall[b, 4:5, :] += column_sum(dr)

        loop(rows // ROWS, norm_two, 2)
        act(b, N1).start()
        act(b, INV1).start()
        if b == 1:
            pl.semaphore_wait(barrier, BITS + 1)
        point()
        for j in range(count):
            ring(b, G, j).wait()
            turned[...] = gring[j % wide].T
            if j + wide < count:
                ring(b, G, j + wide).start()
            product(low_buf, 0, lambda piece: (piece % count, j * (PARTS // count) + piece // count))
            point()
        for c in range(count):
            hand_over(b, 8 + c, c)
        act(b, HLOW).wait()
        turned[...] = lhs[...].T
        act(b, O).start()

        for j in range(count):
            down = weight_next()
            ring(b, SLOPE, j).wait()

            def narrow(t):
                cols = tile_of(t)
                dz = dot_nt(low_buf[...], down[cols, :]) * sring[j % wide, :, cols].astype(F32)
                dsmall[b, 8 + j : 9 + j, cols] = column_sum(dz)
                dz_buf[:, cols] = dz.astype(BF)

            loop(width // TILE, narrow, 3)
            weight_done()
            if j + wide < count:
                ring(b, SLOPE, j + wide).start()
            point()
            finish(b, 8 + j, j)
            product(dz_buf, 0, lambda piece: (j, piece))
            hand_over(b, 4 + j, j)
            point()
            up = weight_next()

            def widen(t):
                cols = tile_of(t)
                acc[:, cols] += dot_nt(dz_buf[...], up[cols, :])

            loop(width // TILE, widen, 3)
            weight_done()
            point()
            if j > 0:
                finish(b, 3 + j, j - 1)
        act(b, N1).wait()
        act(b, INV1).wait()

        def norm_one(i):
            r = tile_of(i, ROWS)
            gradient = acc[r, :]
            normed = norm_buf[r, :]
            dr = norm_back(gradient * small[6:7, :], normed, inv_buf[r, 0:1])
            acc[r, :] = dr
            low_buf[r, :] = dr.astype(BF)
            dsmall[b, 6:7, :] += column_sum(gradient * normed)
            dsmall[b, 3:4, :] += column_sum(gradient)
            dsmall[b, 2:3, :] += column_sum(dr)

        loop(rows // ROWS, norm_one, 2)
        finish(b, 7, 3)
        point()
        act(b, O).wait()
        turned[...] = lhs[...].T
        act(b, X).start()
        product(low_buf, 0, lambda piece: (0, piece))
        hand_over(b, 3, 0)
        point()
        mixer = weight_next()

        def mix(t):
            cols = tile_of(t)
            cot_buf[:, cols] = dot_nt(low_buf[...], mixer[cols, :]).astype(BF)

        loop(width // TILE, mix, 3)
        weight_done()
        act(b, QKV).wait()
        act(b, LSE).wait()
        point()

        def attend(pair):
            here = tile_of(pair, 128)
            key_cols = pl.ds(pl.multiple_of(width + pair * 128, 128), 128)
            value_cols = pl.ds(pl.multiple_of(2 * width + pair * 128, 128), 128)
            queries, keys, values = qkv_buf[:, here], qkv_buf[:, key_cols], qkv_buf[:, value_cols]
            grad = cot_buf[:, here]
            masks = lane_masks((rows, 128))
            dq, dk, dv = [], 0.0, 0.0
            for h in range(2):
                head_queries = jnp.where(masks[h], queries, jnp.zeros_like(queries))
                head_grad = jnp.where(masks[h], grad, jnp.zeros_like(grad))
                scores = dot_nt(keys, head_queries) + mask_ref[...]
                weight = jnp.exp(scores - lse_buf[pair, pl.ds(h, 1), :])
                dweight = dot_nt(values, head_grad)
                delta = jnp.sum(weight * dweight, axis=0, keepdims=True)
                dscore = (weight * (dweight - delta)).astype(BF)
                dq.append(dot_tn(keys, dscore)[h * HEAD : (h + 1) * HEAD])
                dk = dk + dot_nn(dscore, head_queries)
                dv = dv + dot_nn(weight.astype(BF), head_grad)
            dq = jnp.concatenate(dq, axis=0).T * (HEAD ** -0.5)
            dsmall[b, 0:1, here] = column_sum(dq)
            dsmall[b, 1:2, here] = column_sum(dv)
            qkv_buf[:, here] = dq.astype(BF)
            qkv_buf[:, key_cols] = dk.astype(BF)
            qkv_buf[:, value_cols] = dv.astype(BF)

        for third in range(3):
            loop(HEADS // 6, lambda i: attend(third * (HEADS // 6) + i), 2)
            if third == 0:
                finish(b, 3, 0)
            point()
        act(b, X).wait()
        turned[...] = lhs[...].T
        if b == 1:
            act(0, HLOW).start()
            first_loads(0)
        point()

        for j in range(3):
            product(qkv_buf, j * width, lambda piece: (1 + j, piece))
            hand_over(b, j, 1 + j)
            point()
            block_weight = weight_next()

            def project(t):
                cols = tile_of(t)
                dx = acc[:, cols] + dot_nt(qkv_buf[:, j * width : (j + 1) * width], block_weight[cols, :])
                if j < 2:
                    acc[:, cols] = dx
                elif b == 1:
                    dx_ref[:, cols] = dx
                else:
                    dx_ref[:, cols] = dx + jnp.where(first_ref[:, 0:1] > 0.5, 0.0, dx_ref[:, cols])

            loop(width // TILE, project, 3)
            weight_done()
            point()
            if j > 0:
                finish(b, j - 1, j)
        finish(b, 2, 3)

    def own_grad():
        return pltpu.make_async_copy(dx_ref, grad_input.at[mine], grad_sem.at[0])

    def sent_grad():
        return pltpu.make_async_remote_copy(
            src_ref=dx_ref, dst_ref=grad_input.at[mine], send_sem=grad_sem.at[1], recv_sem=grad_sem.at[2],
            device_id={"section": 1 - sec}, device_id_type=MESH,
        )

    own_grad().start()
    sent_grad().start()

    def small_exchange(phase):
        target = {"section": 1 - sec} if phase == 0 else {"dp": me ^ (1 << (phase - 1))}
        source = dsmall.at[1 - sec] if phase == 0 else small_sum.at[phase]
        return pltpu.make_async_remote_copy(
            src_ref=source, dst_ref=small_in.at[phase], send_sem=small_send.at[phase], recv_sem=small_recv.at[phase],
            device_id=target, device_id_type=MESH,
        )

    def small_take(phase):
        small_exchange(phase).wait()
        before = dsmall[sec] if phase == 0 else small_sum[phase]
        if phase < BITS:
            small_sum[phase + 1] = before + small_in[phase]
            small_exchange(phase + 1).start()
        else:
            sums = before + small_in[phase]
            for part in range(PARTS):
                cut = slice(part * share, (part + 1) * share)
                line, start = part * count // PARTS, (part % (PARTS // count)) * count * share

                @pl.when(me == part)
                def _():
                    out_biases[...] = sums[0:6, cut]
                    out_gains[...] = sums[6:8, cut]
                    out_upb[...] = sums[8 + line : 9 + line, start : start + count * share]

    small_exchange(0).start()
    left = [[step for step in steps if step[0] >= points[0] and owner(step[1], step[2]) == core] for core in range(2)]
    for phase in range(BITS + 1):
        run_steps(left[0][:3] + left[1][:3])
        left = [left[0][3:], left[1][3:]]
        small_take(phase)
    run_steps(left[0] + left[1])
    for chunk in SEQUENCE[1::2]:
        bring(chunk).wait()
    own_grad().wait()
    sent_grad().wait()


def backward_sum(kept, hidden, x1, cotangent, cot_theirs, weights, theirs, seg, smalls):
    rows, width = x1.shape
    hidden_width = kept[6].shape[2]
    share = width // PARTS
    chunks = 2 * hidden_width // width + 4
    return pl.pallas_call(
        backward_sum_kernel,
        out_shape=(
            shaped((share, 3 * width)), shaped((share, width)), shaped((share, hidden_width)),
            shaped((hidden_width // PARTS, width)), shaped((6, share)), shaped((2, share)),
            shaped((1, hidden_width // PARTS)), shaped((2 * rows, width)),
        ),
        in_specs=in_hbm(19) + in_vmem(2),
        out_specs=tuple(in_vmem(7) + in_hbm(1)),
        scratch_shapes=[
            pltpu.VMEM((chunks, 2, 2, 2, 2, share, width), BF),
            pltpu.VMEM((SLOTS, 2, 2, 2, 2, share, width), BF),
            pltpu.VMEM((chunks // 2, share, width), F32),
            pltpu.VMEM((chunks, 2, 2, 2, share, width), BF),
            pltpu.VMEM((chunks, 2, 2, share, width), BF),
            pltpu.VMEM((chunks, 2, share, width), BF),
            pltpu.VMEM((chunks, share, width), BF),
            pltpu.VMEM((3, width, width), BF),
            pltpu.VMEM((2, rows, width), BF),
            pltpu.VMEM((2, rows, width), BF),
            pltpu.VMEM((rows, width), BF),
            pltpu.VMEM((width, rows), BF),
            pltpu.VMEM((rows, width), F32),
            pltpu.VMEM((rows, 128), F32),
            pltpu.VMEM((rows, width), BF),
            pltpu.VMEM((rows, 3 * width), BF),
            pltpu.VMEM((HEADS // 2, 2, rows), F32),
            pltpu.VMEM((rows, width), BF),
            pltpu.VMEM((rows, width), BF),
            pltpu.VMEM((rows, width), F32),
            pltpu.VMEM((rows, width), F32),
            pltpu.VMEM((rows, rows), F32),
            pltpu.VMEM((rows, 128), F32),
            pltpu.VMEM((2, 16, width), F32),
            pltpu.VMEM((BITS + 1, 16, width), F32),
            pltpu.VMEM((BITS + 1, 16, width), F32),
            pltpu.SemaphoreType.DMA((chunks,)),
            pltpu.SemaphoreType.DMA((chunks,)),
            pltpu.SemaphoreType.DMA((chunks,)),
            pltpu.SemaphoreType.DMA((chunks,)),
            pltpu.SemaphoreType.DMA((chunks, BITS)),
            pltpu.SemaphoreType.DMA((chunks, BITS)),
            pltpu.SemaphoreType.DMA((BITS + 1,)),
            pltpu.SemaphoreType.DMA((BITS + 1,)),
            pltpu.SemaphoreType.DMA((3,)),
            pltpu.SemaphoreType.DMA((2,)),
            pltpu.SemaphoreType.DMA((2,)),
            pltpu.SemaphoreType.DMA((6,)),
            pltpu.SemaphoreType.DMA((3,)),
        ],
        compiler_params=pltpu.CompilerParams(
            collective_id=0, has_side_effects=True, vmem_limit_bytes=VMEM_BYTES
        ),
        name="backward_sum",
    )(*kept, hidden, x1, cotangent, cot_theirs, *weights, theirs, seg, smalls)


def sum_plainly(pieces, small):
    def scattered(names):
        both = jnp.stack([dot_tn(pieces[b][names[0]], pieces[b][names[1]]) for b in range(2)])
        own = lax.psum_scatter(both, "section", scatter_dimension=0, tiled=False)
        return lax.psum_scatter(own, "dp", scatter_dimension=0, tiled=True)

    own_small = lax.psum(lax.psum_scatter(small, "section", scatter_dimension=0, tiled=False), "dp")
    return tuple(scattered(names) for names in ((0, 1), (2, 3), (4, 5), (6, 7))) + (own_small,)


def hand_out_kernel(count, *refs):
    given, results, held, sems = refs[:count], refs[count : 2 * count], refs[2 * count : 3 * count], refs[3 * count]
    loads = [pltpu.make_async_copy(given[i], held[i], sems.at[0, i]) for i in range(count)]
    stores = [pltpu.make_async_copy(held[i], results[i], sems.at[1, i]) for i in range(count)]
    for load in loads:
        load.start()
    for load, store in zip(loads, stores):
        load.wait()
        store.start()
    for store in stores:
        store.wait()


def hand_out(results):
    count = len(results)
    return pl.pallas_call(
        functools.partial(hand_out_kernel, count),
        out_shape=tuple(shaped(result.shape, result.dtype) for result in results),
        in_specs=in_hbm(count),
        out_specs=tuple(in_hbm(count)),
        scratch_shapes=[pltpu.VMEM(result.shape, result.dtype) for result in results] + [
            pltpu.SemaphoreType.DMA((2, count))
        ],
        compiler_params=pltpu.CompilerParams(vmem_limit_bytes=VMEM_BYTES),
        name="hand_out",
    )(*results)


def swap(value):
    return lax.ppermute(value, "section", [(0, 1), (1, 0)])


def backward_plainly(kept, hidden, x1, cotangent, cot_theirs, weights, theirs, seg, smalls):
    sec, me = lax.axis_index("section"), lax.axis_index("dp")
    share = hidden.shape[1] // lax.axis_size("dp")
    rows, width = x1.shape
    inputs = (lax.dynamic_slice_in_dim(hidden, sec * rows, rows, 0), x1)
    cot_own = lax.dynamic_slice_in_dim(cotangent[0], sec * rows, rows, 0)
    segments = lax.dynamic_index_in_dim(seg, sec, 0, False)
    segr, segc = segments.reshape(1, rows), segments.reshape(rows, 1)
    first = jnp.concatenate([jnp.ones((1,), F32), (segments[1:] != segments[:-1]).astype(F32)]).reshape(rows, 1)
    pairs = []
    for own in weights:
        pairs += [own[0], swap(own[0])]
    pieces, dsmalls, dnext = [None, None], [None, None], x1
    for block in (1, 0):
        qkv, o, lse, n1, inv1, hlow, g, slope, n2, inv2 = (member[block] for member in kept)
        cot = jnp.where(sec == block, cot_own, cot_theirs)
        dnext, dproj, da, dz, df, dsmall, dup = block_backward(
            block, cot, dnext, segr, segc, first, smalls[block], (qkv, o, lse, n1, inv1, slope, n2, inv2), pairs,
        )
        pieces[block] = (inputs[block], dproj, o, da, hlow, dz, g, df)
        dsmalls[block] = jnp.concatenate([dsmall[:8], dup.reshape(-1, width), jnp.zeros((4, width), F32)], axis=0)
    *sums, small = sum_plainly(pieces, jnp.stack(dsmalls))
    columns = lax.dynamic_slice_in_dim(small[:8], me * share, share, 1)
    up_share = kept[6].shape[2] // lax.axis_size("dp")
    upb = lax.dynamic_slice_in_dim(small[8:12].reshape(1, -1), me * up_share, up_share, 1)
    other = swap(dnext)
    grad_input = jnp.concatenate([jnp.where(sec == 0, dnext, other), jnp.where(sec == 0, other, dnext)], axis=0)
    return (*sums, columns[:6], columns[6:], upb, grad_input)


def local(hidden, segment_ids, cotangent, w_qkv, w_out, w_up, w_down, biases, gains, up_bias):
    width = hidden.shape[1]
    assert hidden.shape[0] == 2 * segment_ids.shape[1]
    weights = (w_qkv, w_out, w_up, w_down)
    *kept, x1, states, theirs, cot_theirs, smalls = both_forward(
        hidden, segment_ids, cotangent, weights, biases, gains, up_bias
    )
    fits = lax.axis_size("dp") == PARTS and width % (16 * PARTS) == 0
    backward = backward_sum if fits else backward_plainly
    *totals, upb, grad_input = backward(
        kept, hidden, x1, cotangent, cot_theirs, weights, theirs, segment_ids, smalls
    )
    results = (states, grad_input, *totals, upb)
    if fits:
        results = hand_out(results)
    states, grad_input, *totals, upb = results
    return (states[None], grad_input) + tuple(member[None] for member in totals) + (upb,)


def solution(mesh):
    placed = (
        P("dp", None),
        P("dp", None),
        P("section", "dp", None),
        P("section", None, None),
        P("section", None, None),
        P("section", None, None),
        P("section", None, None),
        P("section", None, None),
        P("section", None, None),
        P("section", None),
    )
    return jax.shard_map(
        local,
        mesh=mesh,
        in_specs=placed,
        out_specs=(
            P("section", "dp", None),
            P("dp", None),
            P("section", "dp", None),
            P("section", "dp", None),
            P("section", "dp", None),
            P("section", "dp", None),
            P("section", None, "dp"),
            P("section", None, "dp"),
            P("section", "dp"),
        ),
        check_vma=False,
    )
```

profile of v0, /device:TPU:0, one launch (start us, length us, event | category | flops | bytes accessed | tf_op | source)
XLA Modules:
  0.0 201.3 jit_solution(6491355233762439503)
XLA Ops:
  0.6 1.3 copy.19.refs_7_
  2.0 51.8 %forward.1 = (bf16[2,512,2304]{2,1,0:T(8,128)(2,1)}, bf16[2,512,768]{2,1,0:T(8,128)(2,1)}, f32[2,6,2,512]{3,2,1,0:T(2,128)}, f32[2,512,768]{2,1,0:T(8,128)}, f32...) custom-call(bf16[1024,768]{1,0:T(8,128)(2,1)} %refs_10_.1, ...), custom_call_target="tpu_custom_call" | custom-call | tf_op jit(solution)/shard_map/forward/pallas_call | solution.py:464
  53.8 141.3 %backward_sum.1 = (f32[48,2304]{1,0:T(8,128)}, f32[48,768]{1,0:T(8,128)}, f32[48,3072]{1,0:T(8,128)}, f32[192,768]{1,0:T(8,128)}, f32[6,48]{1,0:T(8,128)}, /*ind...) custom-call(bf16[2,512,2304]{2,1,0:T(8,128)(2,1)} %get-tuple-element.42.refs_0_, ...), custom_call_target="tpu_custom_call" | custom-call | tf_op jit(solution)/shard_map/backward_sum/pallas_call | solution.py:978
  195.1 4.7 %hand_out.1 = (bf16[1024,768]{1,0:T(8,128)(2,1)}, f32[1024,768]{1,0:T(8,128)}, f32[48,2304]{1,0:T(8,128)}, f32[48,768]{1,0:T(8,128)}, f32[48,3072]{1,0:T(8,128)}...) custom-call(bf16[1024,768]{1,0:T(8,128)(2,1)} %get-tuple-element.41.refs_0_, ...), custom_call_target="tpu_custom_call" | custom-call | tf_op jit(solution)/shard_map/hand_out/pallas_call | solution.py:1060
  199.9 1.3 copy.20
where the time goes:
time: 204 us; the launch traced here: 201 us
  Pallas kernels  198 us (97%)
  local copies, waits for them, and re-layouts  2.6 us (1%)
    pallas_call x1, Pallas kernels, backward_sum(): pl.pallas_call(backward_sum_kernel, out_shape=(shaped((share, 3 * width))...  141 us
    pallas_call x1, Pallas kernels, both_forward(): pl.pallas_call(forward_kernel, out_shape=tuple((shaped((2,) + shape, dtyp...  51.8 us
    pallas_call x1, Pallas kernels, hand_out(): pl.pallas_call(functools.partial(hand_out_kernel, count), out_shape=tuple...  4.74 us

commit v1 on v0

--- a/solution.py
+++ b/solution.py
@@ -169,7 +169,8 @@
     load_x.start()
     for n in range(pieces):
         own_piece(n).start()
-    smalls[sec, 0:6, :] = biases_ref[0]
+    for k in range(biases_ref.shape[0]):
+        smalls[sec, k : k + 1, :] = biases_ref[k]
     smalls[sec, 6:8, :] = gains_ref[0]
     for j in range(count):
         smalls[sec, 8 + j : 9 + j, :] = upb_ref[:, j * width : (j + 1) * width]
@@ -491,7 +492,7 @@
             collective_id=1, has_side_effects=True, vmem_limit_bytes=VMEM_BYTES
         ),
         name="forward",
-    )(hidden, seg, cotangent, *weights, biases, gains, up_bias)
+    )(hidden, seg, cotangent, *weights, jnp.swapaxes(biases, 0, 1), gains, up_bias)
 
 
 def block_backward(block, cot, dnext, segr, segc, first, small, kept, weights):
@@ -521,15 +522,15 @@
 BITS = 4
 PARTS = 1 << BITS
 SLOTS = 4
-SEQUENCE = (8, 9, 10, 11, 4, 5, 6, 7, 3, 0, 1, 2)
-KINDS = ("AFEBABABEFAB", "EFAFEFEFEFAF")
+SEQUENCE = (4, 5, 6, 7, 8, 9, 10, 11, 3, 0, 1, 2)
+KINDS = ("AFEFAFEBABAB", "FFEBEFEFAFEB")
 SCHEDULE = (
-    1428, 1424, 1892, 1888, 2005, 2001, 2108, 2104, 2081, 2184, 2181, 2194, 2572, 2582, 2681, 2775,
-    2771, 2844, 2850, 2973, 3046, 3043, 3145, 3312, 3450, 3431, 3533, 3700, 3838, 3896, 4093, 4160,
-    4181, 4202, 4302, 4319, 4315, 4548, 4566, 4574, 4587, 4657, 4720, 4840, 4857, 4833, 4916, 4913,
-    4946, 4975, 4951, 5016, 5029, 5050, 5026, 5420, 5417, 5589, 5586, 5606, 5699, 5802, 5785, 5779,
-    5772, 5803, 5786, 5819, 5811, 5787, 5773, 5764, 5774, 5765, 5775, 5766, 5767, 5823, 5805, 5782,
-    5788, 5799, 5783, 5760, 5806, 5789, 5768, 5761, 5807, 5790, 5769, 5762, 5791, 5763, 5770, 5771,
+    1792, 1892, 1896, 1985, 2092, 2288, 2388, 2377, 2469, 2466, 2765, 2876, 3064, 3253, 3249, 3242,
+    3334, 3408, 3612, 3630, 3715, 3723, 3815, 4121, 4114, 4184, 4221, 4189, 4276, 4310, 4410, 4624,
+    4628, 4691, 4753, 4766, 4783, 4824, 4853, 4894, 4953, 4913, 4983, 5020, 5013, 5042, 5055, 5083,
+    5216, 5375, 5430, 5508, 5593, 5778, 5800, 5793, 5818, 5786, 5772, 5779, 5811, 5819, 5787, 5801,
+    5773, 5794, 5764, 5802, 5795, 5765, 5803, 5774, 5766, 5775, 5767, 5782, 5789, 5804, 5815, 5783,
+    5797, 5790, 5805, 5760, 5791, 5798, 5806, 5761, 5799, 5768, 5807, 5762, 5769, 5763, 5770, 5771,
 )
 
 
@@ -780,6 +781,56 @@
         if b == 1:
             pl.semaphore_wait(barrier, BITS + 1)
         point()
+        act(b, HLOW).wait()
+        turned[...] = lhs[...].T
+        act(b, O).start()
+
+        for j in range(count):
+            down = weight_next()
+            ring(b, SLOPE, j).wait()
+
+            def narrow(t):
+                cols = tile_of(t)
+                dz = dot_nt(low_buf[...], down[cols, :]) * sring[j % wide, :, cols].astype(F32)
+                dsmall[b, 8 + j : 9 + j, cols] = column_sum(dz)
+                dz_buf[:, cols] = dz.astype(BF)
+
+            loop(width // TILE, narrow, 3)
+            weight_done()
+            if j + wide < count:
+                ring(b, SLOPE, j + wide).start()
+            point()
+            product(dz_buf, 0, lambda piece: (j, piece))
+            hand_over(b, 4 + j, j)
+            point()
+            up = weight_next()
+
+            def widen(t):
+                cols = tile_of(t)
+                acc[:, cols] += dot_nt(dz_buf[...], up[cols, :])
+
+            loop(width // TILE, widen, 3)
+            weight_done()
+            point()
+            if j > 0:
+                finish(b, 3 + j, j - 1)
+        act(b, N1).wait()
+        act(b, INV1).wait()
+
+        def norm_one(i):
+            r = tile_of(i, ROWS)
+            gradient = acc[r, :]
+            normed = norm_buf[r, :]
+            dr = norm_back(gradient * small[6:7, :], normed, inv_buf[r, 0:1])
+            acc[r, :] = dr
+            dz_buf[r, :] = dr.astype(BF)
+            dsmall[b, 6:7, :] += column_sum(gradient * normed)
+            dsmall[b, 3:4, :] += column_sum(gradient)
+            dsmall[b, 2:3, :] += column_sum(dr)
+
+        loop(rows // ROWS, norm_one, 2)
+        finish(b, 7, 3)
+        point()
         for j in range(count):
             ring(b, G, j).wait()
             turned[...] = gring[j % wide].T
@@ -789,68 +840,11 @@
             point()
         for c in range(count):
             hand_over(b, 8 + c, c)
-        act(b, HLOW).wait()
-        turned[...] = lhs[...].T
-        act(b, O).start()
-
-        for j in range(count):
-            down = weight_next()
-            ring(b, SLOPE, j).wait()
-
-            def narrow(t):
-                cols = tile_of(t)
-                dz = dot_nt(low_buf[...], down[cols, :]) * sring[j % wide, :, cols].astype(F32)
-                dsmall[b, 8 + j : 9 + j, cols] = column_sum(dz)
-                dz_buf[:, cols] = dz.astype(BF)
-
-            loop(width // TILE, narrow, 3)
-            weight_done()
-            if j + wide < count:
-                ring(b, SLOPE, j + wide).start()
-            point()
-            finish(b, 8 + j, j)
-            product(dz_buf, 0, lambda piece: (j, piece))
-            hand_over(b, 4 + j, j)
-            point()
-            up = weight_next()
-
-            def widen(t):
-                cols = tile_of(t)
-                acc[:, cols] += dot_nt(dz_buf[...], up[cols, :])
-
-            loop(width // TILE, widen, 3)
-            weight_done()
-            point()
-            if j > 0:
-                finish(b, 3 + j, j - 1)
-        act(b, N1).wait()
-        act(b, INV1).wait()
-
-        def norm_one(i):
-            r = tile_of(i, ROWS)
-            gradient = acc[r, :]
-            normed = norm_buf[r, :]
-            dr = norm_back(gradient * small[6:7, :], normed, inv_buf[r, 0:1])
-            acc[r, :] = dr
-            low_buf[r, :] = dr.astype(BF)
-            dsmall[b, 6:7, :] += column_sum(gradient * normed)
-            dsmall[b, 3:4, :] += column_sum(gradient)
-            dsmall[b, 2:3, :] += column_sum(dr)
-
-        loop(rows // ROWS, norm_one, 2)
-        finish(b, 7, 3)
-        point()
-        act(b, O).wait()
-        turned[...] = lhs[...].T
-        act(b, X).start()
-        product(low_buf, 0, lambda piece: (0, piece))
-        hand_over(b, 3, 0)
-        point()
         mixer = weight_next()
 
         def mix(t):
             cols = tile_of(t)
-            cot_buf[:, cols] = dot_nt(low_buf[...], mixer[cols, :]).astype(BF)
+            cot_buf[:, cols] = dot_nt(dz_buf[...], mixer[cols, :]).astype(BF)
 
         loop(width // TILE, mix, 3)
         weight_done()
@@ -887,8 +881,22 @@
         for third in range(3):
             loop(HEADS // 6, lambda i: attend(third * (HEADS // 6) + i), 2)
             if third == 0:
+                finish(b, 8, 0)
+                finish(b, 9, 1)
+                point()
+                act(b, O).wait()
+                turned[...] = lhs[...].T
+                act(b, X).start()
+                product(dz_buf, 0, lambda piece: (0, piece))
+                hand_over(b, 3, 0)
+                point()
+            elif third == 1:
+                finish(b, 10, 2)
+                finish(b, 11, 3)
+                point()
+            else:
                 finish(b, 3, 0)
-            point()
+                point()
         act(b, X).wait()
         turned[...] = lhs[...].T
         if b == 1:
@@ -953,7 +961,8 @@
 
                 @pl.when(me == part)
                 def _():
-                    out_biases[...] = sums[0:6, cut]
+                    for k in range(out_biases.shape[0]):
+                        out_biases[k] = sums[k : k + 1, cut]
                     out_gains[...] = sums[6:8, cut]
                     out_upb[...] = sums[8 + line : 9 + line, start : start + count * share]
 
@@ -979,7 +988,7 @@
         backward_sum_kernel,
         out_shape=(
             shaped((share, 3 * width)), shaped((share, width)), shaped((share, hidden_width)),
-            shaped((hidden_width // PARTS, width)), shaped((6, share)), shaped((2, share)),
+            shaped((hidden_width // PARTS, width)), shaped((6, 1, share)), shaped((2, share)),
             shaped((1, hidden_width // PARTS)), shaped((2 * rows, width)),
         ),
         in_specs=in_hbm(19) + in_vmem(2),
@@ -1042,10 +1051,16 @@
     return tuple(scattered(names) for names in ((0, 1), (2, 3), (4, 5), (6, 7))) + (own_small,)
 
 
-def hand_out_kernel(count, *refs):
+def hand_out_kernel(cuts, *refs):
+    count = len(cuts)
     given, results, held, sems = refs[:count], refs[count : 2 * count], refs[2 * count : 3 * count], refs[3 * count]
-    loads = [pltpu.make_async_copy(given[i], held[i], sems.at[0, i]) for i in range(count)]
-    stores = [pltpu.make_async_copy(held[i], results[i], sems.at[1, i]) for i in range(count)]
+    loads, stores = [], []
+    for i, cut in enumerate(cuts):
+        size = given[i].shape[0] // cut
+        for part in range(cut):
+            at = pl.ds(part * size, size)
+            loads.append(pltpu.make_async_copy(given[i].at[at], held[i].at[at], sems.at[0, len(loads)]))
+            stores.append(pltpu.make_async_copy(held[i].at[at], results[i].at[at], sems.at[1, len(stores)]))
     for load in loads:
         load.start()
     for load, store in zip(loads, stores):
@@ -1057,13 +1072,14 @@
 
 def hand_out(results):
     count = len(results)
+    cuts = [1] * count
     return pl.pallas_call(
-        functools.partial(hand_out_kernel, count),
+        functools.partial(hand_out_kernel, cuts),
         out_shape=tuple(shaped(result.shape, result.dtype) for result in results),
         in_specs=in_hbm(count),
         out_specs=tuple(in_hbm(count)),
         scratch_shapes=[pltpu.VMEM(result.shape, result.dtype) for result in results] + [
-            pltpu.SemaphoreType.DMA((2, count))
+            pltpu.SemaphoreType.DMA((2, sum(cuts)))
         ],
         compiler_params=pltpu.CompilerParams(vmem_limit_bytes=VMEM_BYTES),
         name="hand_out",
@@ -1101,7 +1117,7 @@
     upb = lax.dynamic_slice_in_dim(small[8:12].reshape(1, -1), me * up_share, up_share, 1)
     other = swap(dnext)
     grad_input = jnp.concatenate([jnp.where(sec == 0, dnext, other), jnp.where(sec == 0, other, dnext)], axis=0)
-    return (*sums, columns[:6], columns[6:], upb, grad_input)
+    return (*sums, columns[:6][:, None], columns[6:], upb, grad_input)
 
 
 def local(hidden, segment_ids, cotangent, w_qkv, w_out, w_up, w_down, biases, gains, up_bias):
@@ -1119,8 +1135,9 @@
     results = (states, grad_input, *totals, upb)
     if fits:
         results = hand_out(results)
-    states, grad_input, *totals, upb = results
-    return (states[None], grad_input) + tuple(member[None] for member in totals) + (upb,)
+    states, grad_input, *products, bias_sums, gain_sums, upb = results
+    products = tuple(member[None] for member in products)
+    return (states[None], grad_input) + products + (jnp.swapaxes(bias_sums, 0, 1), gain_sums[None], upb)
 
 
 def solution(mesh):

time: 204 us -> 200 us (0.980)
  local copies, waits for them, and re-layouts: 2.6 us -> 0 us
    unnamed x2 -> x0, local copies, waits for them, and re-layouts: 2.6 us -> none
where the time goes in v1:
time: 200 us; the launch traced here: 197 us
  Pallas kernels  197 us (98%)
    pallas_call x1, Pallas kernels, backward_sum(): pl.pallas_call(backward_sum_kernel, out_shape=(shaped((share, 3 * width))...  140 us
    pallas_call x1, Pallas kernels, both_forward(): pl.pallas_call(forward_kernel, out_shape=tuple((shaped((2,) + shape, dtyp...  51.8 us
    pallas_call x1, Pallas kernels, hand_out(): pl.pallas_call(functools.partial(hand_out_kernel, cuts), out_shape=tuple(...  4.74 us

profile of v1, /device:TPU:0, one launch (start us, length us, event | category | flops | bytes accessed | tf_op | source)
XLA Modules:
  0.0 197.5 jit_solution(6923420426293898391)
XLA Ops:
  0.6 51.8 %forward.1 = (bf16[2,512,2304]{2,1,0:T(8,128)(2,1)}, bf16[2,512,768]{2,1,0:T(8,128)(2,1)}, f32[2,6,2,512]{3,2,1,0:T(2,128)}, f32[2,512,768]{2,1,0:T(8,128)}, f32...) custom-call(bf16[1024,768]{1,0:T(8,128)(2,1)} %refs_10_.1, ...), custom_call_target="tpu_custom_call" | custom-call | tf_op jit(solution)/shard_map/forward/pallas_call | solution.py:465
  52.4 140.1 %backward_sum.1 = (f32[48,2304]{1,0:T(8,128)}, f32[48,768]{1,0:T(8,128)}, f32[48,3072]{1,0:T(8,128)}, f32[192,768]{1,0:T(8,128)}, f32[6,1,48]{2,1,0:T(1,128)}, /...) custom-call(bf16[2,512,2304]{2,1,0:T(8,128)(2,1)} %get-tuple-element.42.refs_0_, ...), custom_call_target="tpu_custom_call" | custom-call | tf_op jit(solution)/shard_map/backward_sum/pallas_call | solution.py:987
  192.5 4.7 %hand_out.1 = (bf16[1024,768]{1,0:T(8,128)(2,1)}, f32[1024,768]{1,0:T(8,128)}, f32[48,2304]{1,0:T(8,128)}, f32[48,768]{1,0:T(8,128)}, f32[48,3072]{1,0:T(8,128)}...) custom-call(bf16[1024,768]{1,0:T(8,128)(2,1)} %get-tuple-element.41.refs_0_, ...), custom_call_target="tpu_custom_call" | custom-call | tf_op jit(solution)/shard_map/hand_out/pallas_call | solution.py:1076

commit v2 on v1

--- a/solution.py
+++ b/solution.py
@@ -16,7 +16,7 @@
 MESH = pl.DeviceIdType.MESH
 BF = jnp.bfloat16
 F32 = jnp.float32
-TILE = 256
+TILE = 768
 ROWS = 128
 VMEM_BYTES = 60 * 1024 * 1024
 
@@ -218,7 +218,7 @@
                     value = value + small[1:2, cols]
                 qkv_buf[:, there] = value.astype(BF)
 
-            loop(width // TILE, project, 3)
+            loop(width // TILE, project, width // TILE)
         store(b, QKV)
         free(b, O, LSE)
 
@@ -246,7 +246,7 @@
             cols = tile_of(t)
             res[:, cols] = x_buf[:, cols].astype(F32) + (dot_nn(o_buf[...], mixer[:, cols]) + small[2:3, cols])
 
-        loop(width // TILE, mix, 3)
+        loop(width // TILE, mix, width // TILE)
         free(b, N1, INV1, HLOW)
 
         def norm_one(i):
@@ -272,16 +272,27 @@
                 g_buf[:, there] = (z * half).astype(BF)
                 slope_buf[:, there] = (half + z * jnp.exp(-0.5 * z * z) * INV_ROOT_TAU).astype(BF)
 
-            loop(width // TILE, widen, 3)
+            loop(width // TILE, widen, width // TILE)
         store(b, G, SLOPE)
-        for j in range(count):
+        downs = [piece(b, 4 + count + j) for j in range(count)] if b == 1 else []
+        for j in range(count if b == 0 else 0):
             down = piece(b, 4 + count + j)
 
             def narrow(t):
                 cols = tile_of(t)
                 h_buf[:, cols] += dot_nn(g_buf[:, j * width : (j + 1) * width], down[:, cols])
 
-            loop(width // TILE, narrow, 3)
+            loop(width // TILE, narrow, width // TILE)
+
+        def narrow_whole(t):
+            cols = tile_of(t)
+            value = h_buf[:, cols]
+            for j, down in enumerate(downs):
+                value = value + dot_nn(g_buf[:, j * width : (j + 1) * width], down[:, cols])
+            h_buf[:, cols] = value
+
+        if b == 1:
+            loop(width // TILE, narrow_whole, width // TILE)
         free(b, N2, INV2)
 
         def norm_two(i):
@@ -380,7 +391,7 @@
         cols = tile_of(j)
         dh_ref[:, cols] = dr_ref[:, cols] + dot_nt(dz_ref[...], wup[cols, :])
 
-    loop(width // TILE, widen, 3)
+    loop(width // TILE, widen, width // TILE)
 
     def norm_one(i):
         r = tile_of(i, ROWS)
@@ -400,7 +411,7 @@
         cols = tile_of(j)
         do_ref[:, cols] = dot_nt(da_ref[...], wout[cols, :]).astype(BF)
 
-    loop(width // TILE, mix, 3)
+    loop(width // TILE, mix, width // TILE)
 
     def attend(pair):
         here = tile_of(pair, 128)
@@ -438,7 +449,7 @@
             dx = dx + jnp.where(first_ref[...] > 0.5, 0.0, dnext_ref[:, cols])
         dx_ref[:, cols] = dx
 
-    loop(width // TILE, project, 3)
+    loop(width // TILE, project, width // TILE)
 
 
 def in_vmem(count):
@@ -729,7 +740,7 @@
                 slot, part = put(piece)
                 slots[(slot,) + place(part) + (slice(None), cols)] = result[piece * share : (piece + 1) * share]
 
-        loop(width // TILE, one, 3)
+        loop(width // TILE, one, width // TILE)
 
     def first_loads(b):
         @pl.when(sec == b)
@@ -795,7 +806,7 @@
                 dsmall[b, 8 + j : 9 + j, cols] = column_sum(dz)
                 dz_buf[:, cols] = dz.astype(BF)
 
-            loop(width // TILE, narrow, 3)
+            loop(width // TILE, narrow, width // TILE)
             weight_done()
             if j + wide < count:
                 ring(b, SLOPE, j + wide).start()
@@ -809,7 +820,7 @@
                 cols = tile_of(t)
                 acc[:, cols] += dot_nt(dz_buf[...], up[cols, :])
 
-            loop(width // TILE, widen, 3)
+            loop(width // TILE, widen, width // TILE)
             weight_done()
             point()
             if j > 0:
@@ -846,7 +857,7 @@
             cols = tile_of(t)
             cot_buf[:, cols] = dot_nt(dz_buf[...], mixer[cols, :]).astype(BF)
 
-        loop(width // TILE, mix, 3)
+        loop(width // TILE, mix, width // TILE)
         weight_done()
         act(b, QKV).wait()
         act(b, LSE).wait()
@@ -920,7 +931,7 @@
                 else:
                     dx_ref[:, cols] = dx + jnp.where(first_ref[:, 0:1] > 0.5, 0.0, dx_ref[:, cols])
 
-            loop(width // TILE, project, 3)
+            loop(width // TILE, project, width // TILE)
             weight_done()
             point()
             if j > 0:

time: 200 us -> 200 us (level)
  no operation moved by 1% of the time
where the time goes in v2:
time: 200 us; the launch traced here: 197 us
  Pallas kernels  196 us (98%)
    pallas_call x1, Pallas kernels, backward_sum(): pl.pallas_call(backward_sum_kernel, out_shape=(shaped((share, 3 * width))...  140 us
    pallas_call x1, Pallas kernels, both_forward(): pl.pallas_call(forward_kernel, out_shape=tuple((shaped((2,) + shape, dtyp...  51.6 us
    pallas_call x1, Pallas kernels, hand_out(): pl.pallas_call(functools.partial(hand_out_kernel, cuts), out_shape=tuple(...  4.74 us

profile of v2, /device:TPU:0, one launch (start us, length us, event | category | flops | bytes accessed | tf_op | source)
XLA Modules:
  0.0 197.3 jit_solution(4298304662205923025)
XLA Ops:
  0.6 51.6 %forward.1 = (bf16[2,512,2304]{2,1,0:T(8,128)(2,1)}, bf16[2,512,768]{2,1,0:T(8,128)(2,1)}, f32[2,6,2,512]{3,2,1,0:T(2,128)}, f32[2,512,768]{2,1,0:T(8,128)}, f32...) custom-call(bf16[1024,768]{1,0:T(8,128)(2,1)} %refs_10_.1, ...), custom_call_target="tpu_custom_call" | custom-call | tf_op jit(solution)/shard_map/forward/pallas_call | solution.py:476
  52.2 140.1 %backward_sum.1 = (f32[48,2304]{1,0:T(8,128)}, f32[48,768]{1,0:T(8,128)}, f32[48,3072]{1,0:T(8,128)}, f32[192,768]{1,0:T(8,128)}, f32[6,1,48]{2,1,0:T(1,128)}, /...) custom-call(bf16[2,512,2304]{2,1,0:T(8,128)(2,1)} %get-tuple-element.42.refs_0_, ...), custom_call_target="tpu_custom_call" | custom-call | tf_op jit(solution)/shard_map/backward_sum/pallas_call | solution.py:998
  192.4 4.7 %hand_out.1 = (bf16[1024,768]{1,0:T(8,128)(2,1)}, f32[1024,768]{1,0:T(8,128)}, f32[48,2304]{1,0:T(8,128)}, f32[48,768]{1,0:T(8,128)}, f32[48,3072]{1,0:T(8,128)}...) custom-call(bf16[1024,768]{1,0:T(8,128)(2,1)} %get-tuple-element.41.refs_0_, ...), custom_call_target="tpu_custom_call" | custom-call | tf_op jit(solution)/shard_map/hand_out/pallas_call | solution.py:1087
